TPU v7x, 256 devices: a whole 4x4x8 slice. The times are simulated.
256 devices in a mesh: dp: 2 (over core), dom: 128 (over y, z, x).
Axes of the slice: x: 4, y: 4, z: 8, core: 2. Of those that a mesh axis runs over, the one named last changes fastest.
Arguments:
- features: bfloat16 [2, 49152, 512], P('dp', 'dom'), may hold values from -12 to 12
- tile_mask: int32 [2, 384, 18], P('dp', 'dom'), may hold values from 0 to 1, as said below
- cotangent: bfloat16 [2, 49152, 512], P('dp', 'dom'), may hold values from -6 to 6
- w_query: bfloat16 [512, 512], replicated, may hold values from -1 to 1
- w_key: bfloat16 [512, 512], replicated, may hold values from -1 to 1
- w_value: bfloat16 [512, 512], replicated, may hold values from -0.25 to 0.25
- w_out: bfloat16 [512, 512], replicated, may hold values from -0.25 to 0.25
Outputs:
- attended: bfloat16 [2, 49152, 512], P('dp', 'dom')
- grad_features: bfloat16 [2, 49152, 512], P('dp', 'dom')
- grad_query: float32 [512, 512], replicated
- grad_key: float32 [512, 512], replicated
- grad_value: float32 [512, 512], replicated
- grad_out: float32 [512, 512], replicated
Inputs may be any that keep to these rules, and one draw needn't show every extreme that they name: `tile_mask`: 0 or 1; the share of ones differs between tile groups, from about a quarter to all.
All inputs are finite; a program needn't handle non-finite values.
Results may differ from a plain program's by a relative error of at most 0.023.
Values may be sent and summed in bfloat16 or wider, within the bound.
A program may use at most 128 MiB of HBM per device.

v0:
```python
import jax
import jax.numpy as jnp
from jax import lax
from jax.sharding import PartitionSpec as P

HEADS = 8
HEAD_DIM = 64
TILE = 128
TILE_DEV = 3
NB = 3
CANDT = 18


def with_halo(block, sides, width):
    for axis, dim in sides:
        count = lax.axis_size(axis)
        forward = [(i, i + 1) for i in range(count - 1)]
        forward.append((count - 1, 0))
        backward = [(target, source) for source, target in forward]
        low = lax.ppermute(
            lax.slice_in_dim(block, block.shape[dim] - width, None, axis=dim), axis, forward
        )
        high = lax.ppermute(lax.slice_in_dim(block, 0, width, axis=dim), axis, backward)
        block = jnp.concatenate([low, block, high], axis=dim)
    return block


def from_partner(value, axis, distance):
    mask = 2**distance
    pairs = [(source, source ^ mask) for source in range(lax.axis_size(axis))]
    return lax.ppermute(value, axis, pairs)


def candidate_blocks(block):
    block_rows = block.shape[0]
    near = with_halo(block, (("dom", 0),), block_rows)
    pieces = [block, near[:block_rows], near[2 * block_rows :]]
    levels = lax.axis_size("dom").bit_length() - 1
    for bit_step in range(NB):
        pieces.append(from_partner(block, "dom", levels - 1 - bit_step))
    return pieces


def returned_sum(grad_parts):
    block_rows = grad_parts.shape[1]
    outgoing = jnp.concatenate([grad_parts[1], grad_parts[2]], 0)
    returned = with_halo(outgoing, (("dom", 0),), block_rows)
    summed = grad_parts[0] + returned[:block_rows] + returned[3 * block_rows :]
    levels = lax.axis_size("dom").bit_length() - 1
    for bit_step in range(NB):
        summed = summed + from_partner(grad_parts[3 + bit_step], "dom", levels - 1 - bit_step)
    return summed


def joined(stacked_parts, width_all):
    return jnp.transpose(stacked_parts, (1, 0, 2)).reshape(stacked_parts.shape[1], width_all)


def per_device(features, tile_mask, cotangent, w_query, w_key, w_value, w_out):
    node_rows = features[0]
    block_rows = node_rows.shape[0]
    width_all = node_rows.shape[1]
    highest = lax.Precision.HIGHEST
    factor = HEAD_DIM ** (-0.5)
    w_both = jnp.concatenate([w_key, w_value], 1)
    q_rows = jnp.dot(node_rows, w_query, preferred_element_type=jnp.float32).astype(jnp.bfloat16)
    kv_rows = jnp.dot(node_rows, w_both, preferred_element_type=jnp.float32).astype(jnp.bfloat16)
    cand_kv = jnp.concatenate(candidate_blocks(kv_rows), 0)
    key_count = cand_kv.shape[0]
    keys_all = cand_kv[:, :width_all]
    values_all = cand_kv[:, width_all:]
    own_tile = jnp.arange(CANDT)[None, :] == jnp.arange(TILE_DEV)[:, None]
    live_tiles = (tile_mask[0] == 1) | own_tile
    masking = jnp.where(live_tiles, 0.0, -1e30).astype(jnp.float32)
    cot_rows = cotangent[0]
    grad_o = jnp.dot(cot_rows, w_out.T, preferred_element_type=jnp.float32).astype(jnp.bfloat16)
    pair_cols = 2 * HEAD_DIM

    def head_pair(pair_index):
        col_start = pair_index * pair_cols
        q_pair = lax.dynamic_slice_in_dim(q_rows, col_start, pair_cols, 1).reshape(
            block_rows, 2, HEAD_DIM
        )
        k_pair = lax.dynamic_slice_in_dim(keys_all, col_start, pair_cols, 1).reshape(
            key_count, 2, HEAD_DIM
        )
        v_pair = lax.dynamic_slice_in_dim(values_all, col_start, pair_cols, 1).reshape(
            key_count, 2, HEAD_DIM
        )
        g_pair = lax.dynamic_slice_in_dim(grad_o, col_start, pair_cols, 1).reshape(
            block_rows, 2, HEAD_DIM
        )
        scores = (
            jnp.einsum("rhd,chd->hrc", q_pair, k_pair, preferred_element_type=jnp.float32) * factor
        )
        scores = scores.reshape(2, TILE_DEV, TILE, CANDT, TILE) + masking[None, :, None, :, None]
        scores = scores.reshape(2, block_rows, key_count)
        row_max = jnp.max(scores, axis=2, keepdims=True)
        exp_vals = jnp.exp(scores - row_max)
        prob_f32 = exp_vals / jnp.sum(exp_vals, axis=2, keepdims=True)
        prob_bf = prob_f32.astype(jnp.bfloat16)
        out_pair = jnp.einsum(
            "hrc,chd->rhd", prob_bf, v_pair, preferred_element_type=jnp.float32
        ).astype(jnp.bfloat16)
        grad_prob = jnp.einsum("rhd,chd->hrc", g_pair, v_pair, preferred_element_type=jnp.float32)
        row_delta = jnp.einsum(
            "rhd,rhd->hr", g_pair.astype(jnp.float32), out_pair.astype(jnp.float32)
        )
        grad_score = (prob_f32 * (grad_prob - row_delta[:, :, None]) * factor).astype(jnp.bfloat16)
        gq_pair = jnp.einsum(
            "hrc,chd->rhd", grad_score, k_pair, preferred_element_type=jnp.float32
        ).reshape(block_rows, pair_cols)
        gk_pair = jnp.einsum(
            "hrc,rhd->chd", grad_score, q_pair, preferred_element_type=jnp.float32
        ).reshape(key_count, pair_cols)
        gv_pair = jnp.einsum(
            "hrc,rhd->chd", prob_bf, g_pair, preferred_element_type=jnp.float32
        ).reshape(key_count, pair_cols)
        return (out_pair.reshape(block_rows, pair_cols), gq_pair, gk_pair, gv_pair)

    stacked = lax.map(head_pair, jnp.arange(HEADS // 2, dtype=jnp.int32))
    out_rows = joined(stacked[0], width_all)
    grad_q = joined(stacked[1], width_all)
    grad_k = joined(stacked[2], width_all)
    grad_v = joined(stacked[3], width_all)
    attended = jnp.dot(out_rows, w_out, preferred_element_type=jnp.float32).astype(jnp.bfloat16)
    grad_parts = jnp.concatenate([grad_k, grad_v], 1).reshape(3 + NB, block_rows, 2 * width_all)
    w_both32 = w_both.astype(jnp.float32)
    rows_f32 = node_rows.astype(jnp.float32)
    own_grad = returned_sum(grad_parts)
    kv_dx = jnp.dot(own_grad, w_both32.T, precision=highest)
    g_both = jnp.dot(rows_f32.T, own_grad, precision=highest)
    grad_x = jnp.dot(grad_q, w_query.astype(jnp.float32).T, precision=highest) + kv_dx
    g_query = jnp.dot(rows_f32.T, grad_q, precision=highest)
    g_out = jnp.dot(out_rows.T, cot_rows, preferred_element_type=jnp.float32)
    g_query, g_key, g_value, g_out = lax.psum(
        (g_query, g_both[:, :width_all], g_both[:, width_all:], g_out), ("dp", "dom")
    )
    return (attended[None], grad_x.astype(jnp.bfloat16)[None], g_query, g_key, g_value, g_out)


def solution(mesh):
    in_specs = (
        P("dp", "dom", None),
        P("dp", "dom", None),
        P("dp", "dom", None),
        P(),
        P(),
        P(),
        P(),
    )
    out_specs = (P("dp", "dom", None), P("dp", "dom", None), P(), P(), P(), P())
    return jax.shard_map(
        per_device, mesh=mesh, in_specs=in_specs, out_specs=out_specs, check_vma=False
    )
```

profile of v0, /device:TPU:8, one launch (start us, length us, event | category | flops | bytes accessed | tf_op | source)
XLA Modules:
  0.0 602.2 jit_solution(1646686012757670933)
XLA Ops:
  10.6 2.7 constant_dynamic-update-slice_fusion.11
  13.3 7.2 %collective-permute-start.4 = (bf16[384,1024]{1,0:T(8,128)(2,1)}, bf16[384,1024]{1,0:T(8,128)(2,1)S(1)}, u32[]{:S(2)}, u32[]{:S(2)}) collective-permute-start(bf16[384,1024]{1,0:T(8,128)(2,1)} %get-tuple-element.146), channel_id=1, source_target_pairs={{0,16},{1,17},{2,18},{3,19},{4,20},{5,21},{6,22},{7,23},{8,24},{9,... | collective-permute-start | bytes 2359304 | tf_op jit(solution)/shard_map/ppermute | solution.py:31
  21.0 2.6 collective-permute-start.2
  23.6 3.6 collective-permute-start.1
  28.1 45.5 %collective-permute-done = bf16[384,1024]{1,0:T(8,128)(2,1)} collective-permute-done((bf16[384,1024]{1,0:T(8,128)(2,1)}, bf16[384,1024]{1,0:T(8,128)(2,1)}, u32[]{:S(2)}, u32[]{:S(2)}) %collective-permute-start) | collective-permute-done | bytes 786464 | tf_op jit(solution)/shard_map/ppermute | solution.py:20
  82.8 4.8 fusion.33
  87.6 110.8 %while.16 = (s32[]{:T(128)}, bf16[4,384,128]{1,2,0:T(8,128)(2,1)}, f32[4,384,128]{1,2,0:T(8,128)}, f32[4,2304,128]{1,2,0:T(8,128)}, f32[4,2304,128]{1,2,0:T(8,12...) while((s32[]{:T(128)}, bf16[4,384,128]{1,2,0:T(8,128)(2,1)}, ...), condition=%wide.region_3.4_spmd, body=%wide.region_0.3_spmd.sunk | while | flops 1378665984 | bytes 104414744 | solution.py:121
  94.9 7.1 %fusion.93 = (f32[2,384]{1,0:T(2,128)S(1)}, f32[2,384,2304]{2,1,0:T(8,128)}) fusion(f32[384,2304]{1,0:T(8,128)} %bitcast.143, bf16[384,2,64]{0,2,1:T(8,128)(2,1)S(1)} %bitcast.150, bf16[2304,2,64]{0,2,1:T(8,128)(2,1)S(1)} %bitcast.144), kind=kOutput, calls=%fused_computation.74.clone.1 | convolution fusion | flops 233572608 | bytes 11308032 | tf_op jit(solution)/shard_map/while/body/eval_jaxpr/sub | solution.py:99
  102.0 3.8 fusion.94
  122.6 7.1 %fusion.93 = (f32[2,384]{1,0:T(2,128)S(1)}, f32[2,384,2304]{2,1,0:T(8,128)}) fusion(f32[384,2304]{1,0:T(8,128)} %bitcast.143, bf16[384,2,64]{0,2,1:T(8,128)(2,1)S(1)} %bitcast.150, bf16[2304,2,64]{0,2,1:T(8,128)(2,1)S(1)} %bitcast.144), kind=kOutput, calls=%fused_computation.74.clone.1 | convolution fusion | flops 233572608 | bytes 11308032 | tf_op jit(solution)/shard_map/while/body/eval_jaxpr/sub | solution.py:99
  129.7 3.8 fusion.94
  150.3 7.1 %fusion.93 = (f32[2,384]{1,0:T(2,128)S(1)}, f32[2,384,2304]{2,1,0:T(8,128)}) fusion(f32[384,2304]{1,0:T(8,128)} %bitcast.143, bf16[384,2,64]{0,2,1:T(8,128)(2,1)S(1)} %bitcast.150, bf16[2304,2,64]{0,2,1:T(8,128)(2,1)S(1)} %bitcast.144), kind=kOutput, calls=%fused_computation.74.clone.1 | convolution fusion | flops 233572608 | bytes 11308032 | tf_op jit(solution)/shard_map/while/body/eval_jaxpr/sub | solution.py:99
  157.4 3.8 fusion.94
  178.0 7.1 %fusion.93 = (f32[2,384]{1,0:T(2,128)S(1)}, f32[2,384,2304]{2,1,0:T(8,128)}) fusion(f32[384,2304]{1,0:T(8,128)} %bitcast.143, bf16[384,2,64]{0,2,1:T(8,128)(2,1)S(1)} %bitcast.150, bf16[2304,2,64]{0,2,1:T(8,128)(2,1)S(1)} %bitcast.144), kind=kOutput, calls=%fused_computation.74.clone.1 | convolution fusion | flops 233572608 | bytes 11308032 | tf_op jit(solution)/shard_map/while/body/eval_jaxpr/sub | solution.py:99
  185.1 3.8 fusion.94
  198.5 5.9 fusion.16
  204.4 6.2 %collective-permute-start.6 = (f32[384,1024]{0,1:T(8,128)}, f32[384,1024]{0,1:T(8,128)S(1)}, u32[]{:S(2)}, u32[]{:S(2)}) collective-permute-start(f32[384,1024]{0,1:T(8,128)} %get-tuple-element.137), channel_id=1, source_target_pairs={{1,0},{2,1},{3,2},{4,3},{5,4},{6,5},{7,6},{8,7},{9,8},{10,9},{11,1... | collective-permute-start | bytes 4718600 | tf_op jit(solution)/shard_map/ppermute | solution.py:23
  210.7 2.6 collective-permute-start.7
  213.2 4.3 collective-permute-start.9
  222.3 90.3 %collective-permute-done.5 = f32[384,1024]{0,1:T(8,128)S(1)} collective-permute-done((f32[384,1024]{0,1:T(8,128)}, f32[384,1024]{0,1:T(8,128)S(1)}, u32[]{:S(2)}, u32[]{:S(2)}) %collective-permute-start.5) | collective-permute-done | bytes 1572896 | tf_op jit(solution)/shard_map/ppermute | solution.py:20
  317.7 2.7 fusion.38
  320.4 3.4 fusion.21
  323.8 264.0 %all-reduce.3.cloned.1.call-done = (f32[512,512]{0,1:T(8,128)}, f32[512,512]{0,1:T(8,128)}, f32[512,512]{0,1:T(8,128)}, f32[512,512]{1,0:T(8,128)}) async-done(((f32[512,512]{0,1:T(8,128)}, f32[512,512]{0,1:T(8,128)}, f32[512,512]{0,1:T(8,128)}, f32[512,512]{1,0:T(8,128)}), (f32[512,512]{0,1:T(8,128)}, f32[512,512]{0,1:T(8,128)}, f32[512,512]{0,1:T(8,128)}, ...) | async-done | bytes 4194320 | tf_op jit(solution)/shard_map/psum | solution.py:136
  587.9 2.7 copy.24
  (173 shorter events, 92.5 us)
Async XLA Ops:
  7.2 20.5 %copy-start = (bf16[512,512]{1,0:T(8,128)(2,1)S(1)}, bf16[512,512]{1,0:T(8,128)(2,1)}, u32[]{:S(2)}) copy-start(bf16[512,512]{1,0:T(8,128)(2,1)} %param.15) | copy-start | bytes 1572868
  7.2 20.0 %copy-start.4 = (bf16[1,384,512]{2,1,0:T(8,128)(2,1)S(1)}, bf16[1,384,512]{2,1,0:T(8,128)(2,1)}, u32[]{:S(2)}) copy-start(bf16[1,384,512]{2,1,0:T(8,128)(2,1)} %param.9) | copy-start | bytes 1179652
  7.2 20.0 %copy-start.6 = (bf16[512,512]{1,0:T(8,128)(2,1)S(1)}, bf16[512,512]{1,0:T(8,128)(2,1)}, u32[]{:S(2)}) copy-start(bf16[512,512]{1,0:T(8,128)(2,1)} %param.12) | copy-start | bytes 1572868
  7.2 20.4 %copy-start.14 = (s32[1,3,18]{2,0,1:T(1,128)S(1)}, s32[1,3,18]{2,0,1:T(1,128)}, u32[]{:S(2)}) copy-start(s32[1,3,18]{2,0,1:T(1,128)} %param.10) | copy-start | bytes 652
  7.2 20.4 %copy-start.9 = (bf16[1,384,512]{2,1,0:T(8,128)(2,1)S(1)}, bf16[1,384,512]{2,1,0:T(8,128)(2,1)}, u32[]{:S(2)}) copy-start(bf16[1,384,512]{2,1,0:T(8,128)(2,1)} %param.11) | copy-start | bytes 1179652
  7.2 580.6 %all-reduce.3.cloned.1.call-start = ((), (), s32[]{:S(2)}) async-start(), calls=%async_computation | async-start | bytes 8388608 | tf_op jit(solution)/shard_map/psum | solution.py:136
  13.3 68.6 %collective-permute-start.4 = (bf16[384,1024]{1,0:T(8,128)(2,1)}, bf16[384,1024]{1,0:T(8,128)(2,1)S(1)}, u32[]{:S(2)}, u32[]{:S(2)}) collective-permute-start(bf16[384,1024]{1,0:T(8,128)(2,1)} %get-tuple-element.146), channel_id=1, source_target_pairs={{0,16},{1,17},{2,18},{3,19},{4,20},{5,21},{6,22},{7,23},{8,24},{9,... | collective-permute-start | bytes 2359304 | tf_op jit(solution)/shard_map/ppermute | solution.py:31
  20.5 59.3 %collective-permute-start.3 = (bf16[384,1024]{1,0:T(8,128)(2,1)}, bf16[384,1024]{1,0:T(8,128)(2,1)}, u32[]{:S(2)}, u32[]{:S(2)}) collective-permute-start(bf16[384,1024]{1,0:T(8,128)(2,1)} %get-tuple-element.146), channel_id=1, source_target_pairs={{0,32},{1,33},{2,34},{3,35},{4,36},{5,37},{6,38},{7,39},{8,40},{9,... | collective-permute-start | bytes 2359304 | tf_op jit(solution)/shard_map/ppermute | solution.py:31
  21.0 56.8 %collective-permute-start.2 = (bf16[384,1024]{1,0:T(8,128)(2,1)}, bf16[384,1024]{1,0:T(8,128)(2,1)}, u32[]{:S(2)}, u32[]{:S(2)}) collective-permute-start(bf16[384,1024]{1,0:T(8,128)(2,1)} %get-tuple-element.146), channel_id=1, source_target_pairs={{0,64},{1,65},{2,66},{3,67},{4,68},{5,69},{6,70},{7,71},{8,72},{9,... | collective-permute-start | bytes 2359304 | tf_op jit(solution)/shard_map/ppermute | solution.py:31
  23.6 52.1 %collective-permute-start.1 = (bf16[384,1024]{1,0:T(8,128)(2,1)}, bf16[384,1024]{1,0:T(8,128)(2,1)}, u32[]{:S(2)}, u32[]{:S(2)}) collective-permute-start(bf16[384,1024]{1,0:T(8,128)(2,1)} %get-tuple-element.146), channel_id=1, source_target_pairs={{1,0},{2,1},{3,2},{4,3},{5,4},{6,5},{7,6},{8,7},{9,8},{10,9},{11,1... | collective-permute-start | bytes 2359304 | tf_op jit(solution)/shard_map/ppermute | solution.py:23
  27.2 46.4 %collective-permute-start = (bf16[384,1024]{1,0:T(8,128)(2,1)}, bf16[384,1024]{1,0:T(8,128)(2,1)}, u32[]{:S(2)}, u32[]{:S(2)}) collective-permute-start(bf16[384,1024]{1,0:T(8,128)(2,1)} %get-tuple-element.146), channel_id=1, source_target_pairs={{0,1},{1,2},{2,3},{3,4},{4,5},{5,6},{6,7},{7,8},{8,9},{9,10},{10,1... | collective-permute-start | bytes 2359304 | tf_op jit(solution)/shard_map/ppermute | solution.py:20
  198.4 114.2 %slice-start = ((s8[4718592]{0:T(1024)(128)(4,1)}), s8[4194304]{0:T(1024)(128)(4,1)S(1)}, s32[]{:S(2)}) async-start(s8[4718592]{0:T(1024)(128)(4,1)} %bitcast.156), calls=%async_computation.1 | async-start | bytes 8388608
  198.4 114.2 %slice-start.2 = ((s8[4718592]{0:T(1024)(128)(4,1)}), s8[4194304]{0:T(1024)(128)(4,1)S(1)}, s32[]{:S(2)}) async-start(s8[4718592]{0:T(1024)(128)(4,1)} %bitcast.160), calls=%async_computation.3 | async-start | bytes 8388608
  198.4 20.5 %copy-start.10 = (bf16[1,384,512]{2,1,0:T(8,128)(2,1)S(1)}, bf16[1,384,512]{2,1,0:T(8,128)(2,1)}, u32[]{:S(2)}) copy-start(bf16[1,384,512]{2,1,0:T(8,128)(2,1)} %param.11) | copy-start | bytes 1179652
  198.4 20.5 %copy-start.11 = (bf16[4,384,128]{1,2,0:T(8,128)(2,1)S(1)}, bf16[4,384,128]{1,2,0:T(8,128)(2,1)}, u32[]{:S(2)}) copy-start(bf16[4,384,128]{1,2,0:T(8,128)(2,1)} %get-tuple-element.66) | copy-start | bytes 1179652
  198.4 21.9 %copy-start.5 = (f32[4,384,128]{1,2,0:T(8,128)S(1)}, f32[4,384,128]{1,2,0:T(8,128)}, u32[]{:S(2)}) copy-start(f32[4,384,128]{1,2,0:T(8,128)} %get-tuple-element.67) | copy-start | bytes 2359300
  198.5 114.2 %slice-start.1 = ((s8[4718592]{0:T(1024)(128)(4,1)}), s8[524288]{0:T(1024)(128)(4,1)S(1)}, s32[]{:S(2)}) async-start(s8[4718592]{0:T(1024)(128)(4,1)} %bitcast.156), calls=%async_computation.2 | async-start | bytes 1048576
  198.5 114.2 %slice-start.3 = ((s8[4718592]{0:T(1024)(128)(4,1)}), s8[524288]{0:T(1024)(128)(4,1)S(1)}, s32[]{:S(2)}) async-start(s8[4718592]{0:T(1024)(128)(4,1)} %bitcast.160), calls=%async_computation.4 | async-start | bytes 1048576
  204.4 108.2 %collective-permute-start.5 = (f32[384,1024]{0,1:T(8,128)}, f32[384,1024]{0,1:T(8,128)S(1)}, u32[]{:S(2)}, u32[]{:S(2)}) collective-permute-start(f32[384,1024]{0,1:T(8,128)} %get-tuple-element.136), channel_id=1, source_target_pairs={{0,1},{1,2},{2,3},{3,4},{4,5},{5,6},{6,7},{7,8},{8,9},{9,10},{10,1... | collective-permute-start | bytes 4718600 | tf_op jit(solution)/shard_map/ppermute | solution.py:20
  204.4 108.2 %collective-permute-start.6 = (f32[384,1024]{0,1:T(8,128)}, f32[384,1024]{0,1:T(8,128)S(1)}, u32[]{:S(2)}, u32[]{:S(2)}) collective-permute-start(f32[384,1024]{0,1:T(8,128)} %get-tuple-element.137), channel_id=1, source_target_pairs={{1,0},{2,1},{3,2},{4,3},{5,4},{6,5},{7,6},{8,7},{9,8},{10,9},{11,1... | collective-permute-start | bytes 4718600 | tf_op jit(solution)/shard_map/ppermute | solution.py:23
  210.7 102.0 %collective-permute-start.7 = (f32[384,1024]{0,1:T(8,128)}, f32[384,1024]{0,1:T(8,128)S(1)}, u32[]{:S(2)}, u32[]{:S(2)}) collective-permute-start(f32[384,1024]{0,1:T(8,128)} %get-tuple-element.138), channel_id=1, source_target_pairs={{0,64},{1,65},{2,66},{3,67},{4,68},{5,69},{6,70},{7,71},{8,72},{9,... | collective-permute-start | bytes 4718600 | tf_op jit(solution)/shard_map/ppermute | solution.py:31
  213.2 99.4 %collective-permute-start.9 = (f32[384,1024]{0,1:T(8,128)S(1)}, f32[384,1024]{0,1:T(8,128)S(1)}, u32[]{:S(2)}, u32[]{:S(2)}) collective-permute-start(f32[384,1024]{0,1:T(8,128)S(1)} %get-tuple-element.139), channel_id=1, source_target_pairs={{0,16},{1,17},{2,18},{3,19},{4,20},{5,21},{6,22},{7,23},{8,24},{9,... | collective-permute-start | bytes 4718600 | tf_op jit(solution)/shard_map/ppermute | solution.py:31
  217.5 95.1 %collective-permute-start.8 = (f32[384,1024]{0,1:T(8,128)S(1)}, f32[384,1024]{0,1:T(8,128)S(1)}, u32[]{:S(2)}, u32[]{:S(2)}) collective-permute-start(f32[384,1024]{0,1:T(8,128)S(1)} %get-tuple-element.140), channel_id=1, source_target_pairs={{0,32},{1,33},{2,34},{3,35},{4,36},{5,37},{6,38},{7,39},{8,40},{9,... | collective-permute-start | bytes 4718600 | tf_op jit(solution)/shard_map/ppermute | solution.py:31
  587.9 6.5 %copy-start.12 = (f32[512,512]{1,0:T(8,128)S(1)}, f32[512,512]{1,0:T(8,128)}, u32[]{:S(2)}) copy-start(f32[512,512]{1,0:T(8,128)} %get-tuple-element.276) | copy-start | bytes 3145732
  (15 other events, 39.8 us)
Sparse Core Ops, SparseCore 0:
  316.7 271.1 all-reduce.2
where the time goes:
time: 603 us; the launch traced here: 602 us
  waiting for transfers between devices  400 us (66%)
  local copies, waits for them, and re-layouts  68.6 us (11%)
  matrix products  66.2 us (11%)
  starting transfers between devices  28.4 us (5%)
  other arithmetic  21.8 us (4%)
  between operations  14.3 us (2%)
    psum x1, waiting for transfers between devices, per_device(): lax.psum((g_query, g_both[:, :width_all], g_both[:, width_all:], g_out),...  264 us
    ppermute x2, waiting for transfers between devices, with_halo(): lax.ppermute(lax.slice_in_dim(block, block.shape[dim] - width, None, axis...  136 us
    sub x4, matrix products, head_pair(): exp_vals = jnp.exp(scores - row_max)  28.3 us
    ppermute x6, starting transfers between devices, from_partner(): return lax.ppermute(value, axis, pairs)  18.5 us
    unnamed x41, local copies, waits for them, and re-layouts  18.1 us
    convert_element_type x4, other arithmetic, head_pair(): prob_bf = prob_f32.astype(jnp.bfloat16)  15.3 us
    while x28, local copies, waits for them, and re-layouts  14.3 us
  transfers between devices with their start and end apart: 11, of which 3 were waited for; matrix products, arithmetic and copies ran while one was open for 3% of the time, Pallas kernels for 0%

commit v1 on v0

--- a/solution.py
+++ b/solution.py
@@ -9,6 +9,11 @@
 TILE_DEV = 3
 NB = 3
 CANDT = 18
+
+
+def axis_by_axis(value_2, inner_axis, outer_axis):
+    half = lax.psum(value_2, inner_axis)
+    return lax.psum(half, outer_axis)
 
 
 def with_halo(block, sides, width):
@@ -133,8 +138,8 @@
     grad_x = jnp.dot(grad_q, w_query.astype(jnp.float32).T, precision=highest) + kv_dx
     g_query = jnp.dot(rows_f32.T, grad_q, precision=highest)
     g_out = jnp.dot(out_rows.T, cot_rows, preferred_element_type=jnp.float32)
-    g_query, g_key, g_value, g_out = lax.psum(
-        (g_query, g_both[:, :width_all], g_both[:, width_all:], g_out), ("dp", "dom")
+    g_query, g_key, g_value, g_out = axis_by_axis(
+        (g_query, g_both[:, :width_all], g_both[:, width_all:], g_out), "dp", "dom"
     )
     return (attended[None], grad_x.astype(jnp.bfloat16)[None], g_query, g_key, g_value, g_out)
 

time: 603 us -> 617 us (1.023)
  waiting for transfers between devices: 400 us -> 413 us
    psum x1 -> x2, waiting for transfers between devices: 264 us -> 277 us  [the longest x1 236 us: axis_by_axis(): return lax.psum(half, outer_axis)]
  transfers between devices with their start and end apart: 11 -> 12, of which waited for: 3 -> 4; matrix products, arithmetic and copies ran while one was open for 3% -> 3% of each run, Pallas kernels for 0% -> 0%
where the time goes in v1:
time: 617 us; the launch traced here: 615 us
  waiting for transfers between devices  413 us (67%)
  local copies, waits for them, and re-layouts  68.5 us (11%)
  matrix products  66.2 us (11%)
  starting transfers between devices  28.4 us (5%)
  other arithmetic  21.8 us (4%)
  between operations  14.3 us (2%)
    psum x1, waiting for transfers between devices, axis_by_axis(): return lax.psum(half, outer_axis)  236 us
    ppermute x2, waiting for transfers between devices, with_halo(): lax.ppermute(lax.slice_in_dim(block, block.shape[dim] - width, None, axis...  136 us
    psum x1, waiting for transfers between devices, axis_by_axis(): half = lax.psum(value_2, inner_axis)  41 us
    sub x4, matrix products, head_pair(): exp_vals = jnp.exp(scores - row_max)  28.4 us
    ppermute x6, starting transfers between devices, from_partner(): return lax.ppermute(value, axis, pairs)  18.5 us
    unnamed x41, local copies, waits for them, and re-layouts  18 us
    convert_element_type x4, other arithmetic, head_pair(): prob_bf = prob_f32.astype(jnp.bfloat16)  15.3 us
    while x28, local copies, waits for them, and re-layouts  14.3 us
  transfers between devices with their start and end apart: 12, of which 4 were waited for; matrix products, arithmetic and copies ran while one was open for 3% of the time, Pallas kernels for 0%

profile of v1, /device:TPU:8, one launch (start us, length us, event | category | flops | bytes accessed | tf_op | source)
XLA Modules:
  0.0 615.2 jit_solution(12341521339595849086)
XLA Ops:
  10.6 2.7 constant_dynamic-update-slice_fusion.11
  13.3 7.2 %collective-permute-start.4 = (bf16[384,1024]{1,0:T(8,128)(2,1)}, bf16[384,1024]{1,0:T(8,128)(2,1)S(1)}, u32[]{:S(2)}, u32[]{:S(2)}) collective-permute-start(bf16[384,1024]{1,0:T(8,128)(2,1)} %get-tuple-element.150), channel_id=1, source_target_pairs={{0,16},{1,17},{2,18},{3,19},{4,20},{5,21},{6,22},{7,23},{8,24},{9,... | collective-permute-start | bytes 2359304 | tf_op jit(solution)/shard_map/ppermute | solution.py:36
  23.5 3.6 collective-permute-start.1
  28.1 45.5 %collective-permute-done = bf16[384,1024]{1,0:T(8,128)(2,1)} collective-permute-done((bf16[384,1024]{1,0:T(8,128)(2,1)}, bf16[384,1024]{1,0:T(8,128)(2,1)}, u32[]{:S(2)}, u32[]{:S(2)}) %collective-permute-start) | collective-permute-done | bytes 786464 | tf_op jit(solution)/shard_map/ppermute | solution.py:25
  82.8 4.8 fusion.33
  87.6 110.8 %while.16 = (s32[]{:T(128)}, bf16[4,384,128]{1,2,0:T(8,128)(2,1)}, f32[4,384,128]{1,2,0:T(8,128)}, f32[4,2304,128]{1,2,0:T(8,128)}, f32[4,2304,128]{1,2,0:T(8,12...) while((s32[]{:T(128)}, bf16[4,384,128]{1,2,0:T(8,128)(2,1)}, ...), condition=%wide.region_3.4_spmd, body=%wide.region_0.3_spmd.sunk | while | flops 1378665984 | bytes 104414744 | solution.py:126
  94.8 7.1 %fusion.93 = (f32[2,384]{1,0:T(2,128)S(1)}, f32[2,384,2304]{2,1,0:T(8,128)}) fusion(f32[384,2304]{1,0:T(8,128)} %bitcast.143, bf16[384,2,64]{0,2,1:T(8,128)(2,1)S(1)} %bitcast.150, bf16[2304,2,64]{0,2,1:T(8,128)(2,1)S(1)} %bitcast.144), kind=kOutput, calls=%fused_computation.74.clone.1 | convolution fusion | flops 233572608 | bytes 11308032 | tf_op jit(solution)/shard_map/while/body/eval_jaxpr/sub | solution.py:104
  101.9 3.8 fusion.94
  122.6 7.1 %fusion.93 = (f32[2,384]{1,0:T(2,128)S(1)}, f32[2,384,2304]{2,1,0:T(8,128)}) fusion(f32[384,2304]{1,0:T(8,128)} %bitcast.143, bf16[384,2,64]{0,2,1:T(8,128)(2,1)S(1)} %bitcast.150, bf16[2304,2,64]{0,2,1:T(8,128)(2,1)S(1)} %bitcast.144), kind=kOutput, calls=%fused_computation.74.clone.1 | convolution fusion | flops 233572608 | bytes 11308032 | tf_op jit(solution)/shard_map/while/body/eval_jaxpr/sub | solution.py:104
  129.7 3.8 fusion.94
  150.3 7.1 %fusion.93 = (f32[2,384]{1,0:T(2,128)S(1)}, f32[2,384,2304]{2,1,0:T(8,128)}) fusion(f32[384,2304]{1,0:T(8,128)} %bitcast.143, bf16[384,2,64]{0,2,1:T(8,128)(2,1)S(1)} %bitcast.150, bf16[2304,2,64]{0,2,1:T(8,128)(2,1)S(1)} %bitcast.144), kind=kOutput, calls=%fused_computation.74.clone.1 | convolution fusion | flops 233572608 | bytes 11308032 | tf_op jit(solution)/shard_map/while/body/eval_jaxpr/sub | solution.py:104
  157.4 3.8 fusion.94
  178.0 7.1 %fusion.93 = (f32[2,384]{1,0:T(2,128)S(1)}, f32[2,384,2304]{2,1,0:T(8,128)}) fusion(f32[384,2304]{1,0:T(8,128)} %bitcast.143, bf16[384,2,64]{0,2,1:T(8,128)(2,1)S(1)} %bitcast.150, bf16[2304,2,64]{0,2,1:T(8,128)(2,1)S(1)} %bitcast.144), kind=kOutput, calls=%fused_computation.74.clone.1 | convolution fusion | flops 233572608 | bytes 11308032 | tf_op jit(solution)/shard_map/while/body/eval_jaxpr/sub | solution.py:104
  185.1 3.8 fusion.94
  198.5 5.9 fusion.16
  204.4 6.2 %collective-permute-start.6 = (f32[384,1024]{0,1:T(8,128)}, f32[384,1024]{0,1:T(8,128)S(1)}, u32[]{:S(2)}, u32[]{:S(2)}) collective-permute-start(f32[384,1024]{0,1:T(8,128)} %get-tuple-element.141), channel_id=1, source_target_pairs={{1,0},{2,1},{3,2},{4,3},{5,4},{6,5},{7,6},{8,7},{9,8},{10,9},{11,1... | collective-permute-start | bytes 4718600 | tf_op jit(solution)/shard_map/ppermute | solution.py:28
  210.6 2.6 collective-permute-start.7
  213.2 4.3 collective-permute-start.9
  222.3 90.3 %collective-permute-done.5 = f32[384,1024]{0,1:T(8,128)S(1)} collective-permute-done((f32[384,1024]{0,1:T(8,128)}, f32[384,1024]{0,1:T(8,128)S(1)}, u32[]{:S(2)}, u32[]{:S(2)}) %collective-permute-start.5) | collective-permute-done | bytes 1572896 | tf_op jit(solution)/shard_map/ppermute | solution.py:25
  316.6 41.0 %all-reduce.7.cloned.1.call-done = (f32[512,512]{0,1:T(8,128)}, f32[512,512]{0,1:T(8,128)}, f32[512,512]{0,1:T(8,128)}, f32[512,512]{1,0:T(8,128)}) async-done(((f32[512,512]{0,1:T(8,128)}, f32[512,512]{0,1:T(8,128)}, f32[512,512]{0,1:T(8,128)}, f32[512,512]{1,0:T(8,128)}), (f32[512,512]{0,1:T(8,128)}, f32[512,512]{0,1:T(8,128)}, f32[512,512]{0,1:T(8,128)}, ...) | async-done | bytes 4194320 | tf_op jit(solution)/shard_map/psum | solution.py:15
  358.8 2.7 fusion.38
  361.6 3.4 fusion.21
  365.0 235.9 %all-reduce.5.cloned.1.call-done = (f32[512,512]{0,1:T(8,128)}, f32[512,512]{0,1:T(8,128)}, f32[512,512]{0,1:T(8,128)}, f32[512,512]{1,0:T(8,128)}) async-done(((f32[512,512]{0,1:T(8,128)}, f32[512,512]{0,1:T(8,128)}, f32[512,512]{0,1:T(8,128)}, f32[512,512]{1,0:T(8,128)}), (f32[512,512]{0,1:T(8,128)}, f32[512,512]{0,1:T(8,128)}, f32[512,512]{0,1:T(8,128)}, ...) | async-done | bytes 4194320 | tf_op jit(solution)/shard_map/psum | solution.py:16
  600.9 2.7 copy.24
  (176 shorter events, 95.2 us)
Async XLA Ops:
  7.2 20.5 %copy-start = (bf16[512,512]{1,0:T(8,128)(2,1)S(1)}, bf16[512,512]{1,0:T(8,128)(2,1)}, u32[]{:S(2)}) copy-start(bf16[512,512]{1,0:T(8,128)(2,1)} %param.15) | copy-start | bytes 1572868
  7.2 20.0 %copy-start.4 = (bf16[1,384,512]{2,1,0:T(8,128)(2,1)S(1)}, bf16[1,384,512]{2,1,0:T(8,128)(2,1)}, u32[]{:S(2)}) copy-start(bf16[1,384,512]{2,1,0:T(8,128)(2,1)} %param.9) | copy-start | bytes 1179652
  7.2 20.0 %copy-start.6 = (bf16[512,512]{1,0:T(8,128)(2,1)S(1)}, bf16[512,512]{1,0:T(8,128)(2,1)}, u32[]{:S(2)}) copy-start(bf16[512,512]{1,0:T(8,128)(2,1)} %param.12) | copy-start | bytes 1572868
  7.2 20.4 %copy-start.14 = (s32[1,3,18]{2,0,1:T(1,128)S(1)}, s32[1,3,18]{2,0,1:T(1,128)}, u32[]{:S(2)}) copy-start(s32[1,3,18]{2,0,1:T(1,128)} %param.10) | copy-start | bytes 652
  7.2 20.4 %copy-start.9 = (bf16[1,384,512]{2,1,0:T(8,128)(2,1)S(1)}, bf16[1,384,512]{2,1,0:T(8,128)(2,1)}, u32[]{:S(2)}) copy-start(bf16[1,384,512]{2,1,0:T(8,128)(2,1)} %param.11) | copy-start | bytes 1179652
  7.2 350.4 %all-reduce.7.cloned.1.call-start = ((), (), s32[]{:S(2)}) async-start(), calls=%async_computation.1 | async-start | bytes 8388608 | tf_op jit(solution)/shard_map/psum | solution.py:15
  13.3 68.5 %collective-permute-start.4 = (bf16[384,1024]{1,0:T(8,128)(2,1)}, bf16[384,1024]{1,0:T(8,128)(2,1)S(1)}, u32[]{:S(2)}, u32[]{:S(2)}) collective-permute-start(bf16[384,1024]{1,0:T(8,128)(2,1)} %get-tuple-element.150), channel_id=1, source_target_pairs={{0,16},{1,17},{2,18},{3,19},{4,20},{5,21},{6,22},{7,23},{8,24},{9,... | collective-permute-start | bytes 2359304 | tf_op jit(solution)/shard_map/ppermute | solution.py:36
  20.5 59.3 %collective-permute-start.3 = (bf16[384,1024]{1,0:T(8,128)(2,1)}, bf16[384,1024]{1,0:T(8,128)(2,1)}, u32[]{:S(2)}, u32[]{:S(2)}) collective-permute-start(bf16[384,1024]{1,0:T(8,128)(2,1)} %get-tuple-element.150), channel_id=1, source_target_pairs={{0,32},{1,33},{2,34},{3,35},{4,36},{5,37},{6,38},{7,39},{8,40},{9,... | collective-permute-start | bytes 2359304 | tf_op jit(solution)/shard_map/ppermute | solution.py:36
  21.0 56.7 %collective-permute-start.2 = (bf16[384,1024]{1,0:T(8,128)(2,1)}, bf16[384,1024]{1,0:T(8,128)(2,1)}, u32[]{:S(2)}, u32[]{:S(2)}) collective-permute-start(bf16[384,1024]{1,0:T(8,128)(2,1)} %get-tuple-element.150), channel_id=1, source_target_pairs={{0,64},{1,65},{2,66},{3,67},{4,68},{5,69},{6,70},{7,71},{8,72},{9,... | collective-permute-start | bytes 2359304 | tf_op jit(solution)/shard_map/ppermute | solution.py:36
  23.5 52.1 %collective-permute-start.1 = (bf16[384,1024]{1,0:T(8,128)(2,1)}, bf16[384,1024]{1,0:T(8,128)(2,1)}, u32[]{:S(2)}, u32[]{:S(2)}) collective-permute-start(bf16[384,1024]{1,0:T(8,128)(2,1)} %get-tuple-element.150), channel_id=1, source_target_pairs={{1,0},{2,1},{3,2},{4,3},{5,4},{6,5},{7,6},{8,7},{9,8},{10,9},{11,1... | collective-permute-start | bytes 2359304 | tf_op jit(solution)/shard_map/ppermute | solution.py:28
  27.2 46.4 %collective-permute-start = (bf16[384,1024]{1,0:T(8,128)(2,1)}, bf16[384,1024]{1,0:T(8,128)(2,1)}, u32[]{:S(2)}, u32[]{:S(2)}) collective-permute-start(bf16[384,1024]{1,0:T(8,128)(2,1)} %get-tuple-element.150), channel_id=1, source_target_pairs={{0,1},{1,2},{2,3},{3,4},{4,5},{5,6},{6,7},{7,8},{8,9},{9,10},{10,1... | collective-permute-start | bytes 2359304 | tf_op jit(solution)/shard_map/ppermute | solution.py:25
  198.4 114.3 %slice-start = ((s8[4718592]{0:T(1024)(128)(4,1)}), s8[4194304]{0:T(1024)(128)(4,1)S(1)}, s32[]{:S(2)}) async-start(s8[4718592]{0:T(1024)(128)(4,1)} %bitcast.156), calls=%async_computation.2 | async-start | bytes 8388608
  198.4 114.3 %slice-start.2 = ((s8[4718592]{0:T(1024)(128)(4,1)}), s8[4194304]{0:T(1024)(128)(4,1)S(1)}, s32[]{:S(2)}) async-start(s8[4718592]{0:T(1024)(128)(4,1)} %bitcast.160), calls=%async_computation.4 | async-start | bytes 8388608
  198.4 20.5 %copy-start.10 = (bf16[1,384,512]{2,1,0:T(8,128)(2,1)S(1)}, bf16[1,384,512]{2,1,0:T(8,128)(2,1)}, u32[]{:S(2)}) copy-start(bf16[1,384,512]{2,1,0:T(8,128)(2,1)} %param.11) | copy-start | bytes 1179652
  198.4 20.5 %copy-start.11 = (bf16[4,384,128]{1,2,0:T(8,128)(2,1)S(1)}, bf16[4,384,128]{1,2,0:T(8,128)(2,1)}, u32[]{:S(2)}) copy-start(bf16[4,384,128]{1,2,0:T(8,128)(2,1)} %get-tuple-element.66) | copy-start | bytes 1179652
  198.4 21.9 %copy-start.5 = (f32[4,384,128]{1,2,0:T(8,128)S(1)}, f32[4,384,128]{1,2,0:T(8,128)}, u32[]{:S(2)}) copy-start(f32[4,384,128]{1,2,0:T(8,128)} %get-tuple-element.67) | copy-start | bytes 2359300
  198.4 114.2 %slice-start.1 = ((s8[4718592]{0:T(1024)(128)(4,1)}), s8[524288]{0:T(1024)(128)(4,1)S(1)}, s32[]{:S(2)}) async-start(s8[4718592]{0:T(1024)(128)(4,1)} %bitcast.156), calls=%async_computation.3 | async-start | bytes 1048576
  198.4 114.2 %slice-start.3 = ((s8[4718592]{0:T(1024)(128)(4,1)}), s8[524288]{0:T(1024)(128)(4,1)S(1)}, s32[]{:S(2)}) async-start(s8[4718592]{0:T(1024)(128)(4,1)} %bitcast.160), calls=%async_computation.5 | async-start | bytes 1048576
  204.4 108.2 %collective-permute-start.5 = (f32[384,1024]{0,1:T(8,128)}, f32[384,1024]{0,1:T(8,128)S(1)}, u32[]{:S(2)}, u32[]{:S(2)}) collective-permute-start(f32[384,1024]{0,1:T(8,128)} %get-tuple-element.140), channel_id=1, source_target_pairs={{0,1},{1,2},{2,3},{3,4},{4,5},{5,6},{6,7},{7,8},{8,9},{9,10},{10,1... | collective-permute-start | bytes 4718600 | tf_op jit(solution)/shard_map/ppermute | solution.py:25
  204.4 108.2 %collective-permute-start.6 = (f32[384,1024]{0,1:T(8,128)}, f32[384,1024]{0,1:T(8,128)S(1)}, u32[]{:S(2)}, u32[]{:S(2)}) collective-permute-start(f32[384,1024]{0,1:T(8,128)} %get-tuple-element.141), channel_id=1, source_target_pairs={{1,0},{2,1},{3,2},{4,3},{5,4},{6,5},{7,6},{8,7},{9,8},{10,9},{11,1... | collective-permute-start | bytes 4718600 | tf_op jit(solution)/shard_map/ppermute | solution.py:28
  210.6 102.0 %collective-permute-start.7 = (f32[384,1024]{0,1:T(8,128)}, f32[384,1024]{0,1:T(8,128)S(1)}, u32[]{:S(2)}, u32[]{:S(2)}) collective-permute-start(f32[384,1024]{0,1:T(8,128)} %get-tuple-element.142), channel_id=1, source_target_pairs={{0,64},{1,65},{2,66},{3,67},{4,68},{5,69},{6,70},{7,71},{8,72},{9,... | collective-permute-start | bytes 4718600 | tf_op jit(solution)/shard_map/ppermute | solution.py:36
  213.2 99.4 %collective-permute-start.9 = (f32[384,1024]{0,1:T(8,128)S(1)}, f32[384,1024]{0,1:T(8,128)S(1)}, u32[]{:S(2)}, u32[]{:S(2)}) collective-permute-start(f32[384,1024]{0,1:T(8,128)S(1)} %get-tuple-element.143), channel_id=1, source_target_pairs={{0,16},{1,17},{2,18},{3,19},{4,20},{5,21},{6,22},{7,23},{8,24},{9,... | collective-permute-start | bytes 4718600 | tf_op jit(solution)/shard_map/ppermute | solution.py:36
  217.6 95.1 %collective-permute-start.8 = (f32[384,1024]{0,1:T(8,128)S(1)}, f32[384,1024]{0,1:T(8,128)S(1)}, u32[]{:S(2)}, u32[]{:S(2)}) collective-permute-start(f32[384,1024]{0,1:T(8,128)S(1)} %get-tuple-element.144), channel_id=1, source_target_pairs={{0,32},{1,33},{2,34},{3,35},{4,36},{5,37},{6,38},{7,39},{8,40},{9,... | collective-permute-start | bytes 4718600 | tf_op jit(solution)/shard_map/ppermute | solution.py:36
  316.6 284.3 %all-reduce.5.cloned.1.call-start = ((), (), s32[]{:S(2)}) async-start(), calls=%async_computation | async-start | bytes 8388608 | tf_op jit(solution)/shard_map/psum | solution.py:16
  (16 other events, 46.4 us)
Sparse Core Ops, SparseCore 0:
  316.7 40.9 all-reduce.6
  364.4 236.4 all-reduce.4
